TPU v7x, 32 devices: a whole 2x2x4 slice. The times are simulated.
32 devices in a mesh: dp: 8 (over z, x), ctx: 4 (over y, core).
Axes of the slice: x: 2, y: 2, z: 4, core: 2. Of those that a mesh axis runs over, the one named last changes fastest.
Arguments:
- tokens: bfloat16 [16, 1024, 768], P('dp', 'ctx'), may hold values from -6 to 6
- norm_weight: bfloat16 [768], P('dp'), may hold values from 0.5 to 1.5
- in_weight: bfloat16 [768, 3352], P('dp'), may hold values from -0.21875 to 0.21875
- conv_weight: bfloat16 [4, 1792], P(None, 'dp'), may hold values from -3 to 3
- conv_bias: bfloat16 [1792], P('dp'), may hold values from -3 to 3
- decay_log: float32 [24], replicated, may hold values from 0 to 2.77
- skip_gain: float32 [24], replicated, may hold values from 0.5 to 1.5
- step_bias: float32 [24], replicated, may hold values from -7 to -3
- gated_gain: bfloat16 [1536], P('dp'), may hold values from 0.5 to 1.5
- out_weight: bfloat16 [1536, 768], P('dp'), may hold values from -0.15625 to 0.15625
- cotangent: bfloat16 [16, 1024, 768], P('dp', 'ctx'), may hold values from -6 to 6
Outputs:
- block_output: bfloat16 [16, 1024, 768], P('dp', 'ctx')
- input_grad: bfloat16 [16, 1024, 768], P('dp', 'ctx')
- norm_grad: float32 [768], P('dp')
- in_grad: float32 [768, 3352], P('dp')
- conv_grad: float32 [4, 1792], P(None, 'dp')
- conv_bias_grad: float32 [1792], P('dp')
- decay_log_grad: float32 [24], replicated
- skip_grad: float32 [24], replicated
- step_bias_grad: float32 [24], replicated
- gated_grad: float32 [1536], P('dp')
- out_grad: float32 [1536, 768], P('dp')
All inputs are finite; a program needn't handle non-finite values.
Results may differ from a plain program's by a relative error of at most 0.0091.
Values may be sent and summed in bfloat16 or wider, within the bound.
A program may use at most 192 MiB of HBM per device.

v0:
```python
import jax
import jax.numpy as jnp
from jax import lax
from jax.sharding import PartitionSpec as P

HEADS = 24
HEADDIM = 64
NSTATE = 128
CONV = 4
SPAN = 128
MICRO = 2
INNER = 1536
XBC = 1792


epsilon = 1e-05
highest = lax.Precision.HIGHEST


def passed_along(block, axis, distance):
    devices = range(lax.axis_size(axis))
    route = [(i - distance, i) for i in devices if i - distance in devices]
    return lax.ppermute(block, axis, route)


def carried_in(part, axis, combine, identity, reverse):
    count = lax.axis_size(axis)
    place = lax.axis_index(axis)
    ahead = count - 1 - place if reverse else place
    gathered = jax.tree.map(lambda a: lax.all_gather(a, axis), part)
    state = jax.tree.map(lambda a, e: jnp.zeros_like(a) + jnp.asarray(e, a.dtype), part, identity)

    def one(lap, state):
        source = count - 1 - lap if reverse else lap
        return combine(
            state, jax.tree.map(lambda a: lax.dynamic_index_in_dim(a, source, 0, False), gathered)
        )

    return lax.fori_loop(0, ahead, one, state)


def silu_grad(pre):
    sigma = jax.nn.sigmoid(pre)
    return sigma * (1.0 + pre * (1.0 - sigma))


def combine(earlier, later):
    return (earlier[0] * later[0], later[1] + later[0][:, None, None] * earlier[1])


def chain_fold(carry, member):
    return ((carry[0] * member[0], member[0][:, None, None] * carry[1] + member[1]), None)


def advance(state, member):
    return (member[0][:, None, None] * state + member[1], state)


def retreat(after, member):
    return (member[1] + member[0][:, None, None] * after, after)


def prepare(projected, edge, conv_full, bias_full, decay_log, step_bias):
    pieces = projected.shape[0]
    span_count = pieces // SPAN
    conv_in = projected[:, INNER : INNER + XBC]
    padded = jnp.concatenate([edge, conv_in], axis=0).astype(jnp.float32)
    conv_taps = conv_full.astype(jnp.float32)
    conv_pre = bias_full.astype(jnp.float32) + sum(
        (padded[offset : offset + pieces] * conv_taps[offset] for offset in range(CONV))
    )
    active = jax.nn.silu(conv_pre)
    values = active[:, :INNER].reshape(span_count, SPAN, HEADS, HEADDIM)
    inputs_b = active[:, INNER : INNER + NSTATE].reshape(span_count, SPAN, NSTATE)
    readout = active[:, INNER + NSTATE :].reshape(span_count, SPAN, NSTATE)
    step_pre = projected[:, INNER + XBC :].astype(jnp.float32) + step_bias
    step_size = jax.nn.softplus(step_pre)
    rate_head = -jnp.exp(decay_log)
    step_spans = step_size.reshape(span_count, SPAN, HEADS)
    cumul = jnp.cumsum((step_size * rate_head).reshape(span_count, SPAN, HEADS), axis=1)
    return (padded, conv_pre, values, inputs_b, readout, step_pre, step_size, step_spans, cumul)


def block_terms(cumul, step_spans, scores):
    cumul_heads = jnp.swapaxes(cumul, 1, 2)
    step_heads = jnp.swapaxes(step_spans, 1, 2)
    causal = jnp.tril(jnp.ones((SPAN, SPAN), jnp.bool_))
    decay_mat = jnp.exp(
        jnp.where(causal, cumul_heads[:, :, :, None] - cumul_heads[:, :, None, :], -1e30)
    )
    weights = scores[:, None] * decay_mat * step_heads[:, :, None, :]
    return (decay_mat, step_heads, weights)


def forward(stream_in, all_weights, head_terms):
    norm_full, in_full, conv_full, bias_full, gain_full, out_full = all_weights
    decay_log, skip_gain, step_bias = head_terms
    pieces = stream_in.shape[0]
    stream = stream_in.astype(jnp.float32)
    inv_rms = lax.rsqrt(jnp.mean(stream * stream, axis=-1, keepdims=True) + epsilon)
    normed = (stream * inv_rms * norm_full.astype(jnp.float32)).astype(jnp.bfloat16)
    projected = jnp.dot(normed, in_full, preferred_element_type=jnp.float32).astype(jnp.bfloat16)
    edge = passed_along(projected[pieces - CONV + 1 :, INNER : INNER + XBC], "ctx", 1)
    padded, conv_pre, values, inputs_b, readout, step_pre, step_size, step_spans, cumul = prepare(
        projected, edge, conv_full, bias_full, decay_log, step_bias
    )
    scores = jnp.einsum("ctn,csn->cts", readout, inputs_b, precision=highest)
    decay_mat, step_heads, weights = block_terms(cumul, step_spans, scores)
    intra_out = jnp.einsum("chts,cshp->cthp", weights, values, precision=highest)
    tail_w = jnp.exp(cumul[:, -1:, :] - cumul) * step_spans
    update = jnp.einsum("cshp,csn->chpn", tail_w[..., None] * values, inputs_b, precision=highest)
    span_decay = jnp.exp(cumul[:, -1, :])
    ones_heads = jnp.ones((HEADS,), jnp.float32)
    zero_state = jnp.zeros((HEADS, HEADDIM, NSTATE), jnp.float32)
    piece_total, _ = lax.scan(chain_fold, (ones_heads, zero_state), (span_decay, update))
    entering = carried_in(piece_total, "ctx", combine, (ones_heads, zero_state), False)[1]
    _, starts = lax.scan(advance, entering, (span_decay, update))
    inter_out = jnp.exp(cumul)[..., None] * jnp.einsum(
        "ctn,chpn->cthp", readout, starts, precision=highest
    )
    ssd_out = (intra_out + inter_out).reshape(pieces, HEADS, HEADDIM)
    mixed_out = (ssd_out + skip_gain[:, None] * values.reshape(pieces, HEADS, HEADDIM)).reshape(
        pieces, INNER
    )
    gate_act = jax.nn.silu(projected[:, :INNER].astype(jnp.float32))
    gate_val = mixed_out * gate_act
    gate_rms = lax.rsqrt(jnp.mean(gate_val * gate_val, axis=-1, keepdims=True) + epsilon)
    gated = (gate_val * gate_rms * gain_full.astype(jnp.float32)).astype(jnp.bfloat16)
    branch = jnp.dot(gated, out_full, preferred_element_type=jnp.float32)
    result = (stream + branch).astype(jnp.bfloat16)
    stored = (normed, projected, edge, starts, piece_total[0], mixed_out)
    return (result, stored)


def backward(stream_in, stored, cotan, all_weights, head_terms):
    normed, projected, edge, starts, piece_decay, mixed_out = stored
    norm_full, in_full, conv_full, bias_full, gain_full, out_full = all_weights
    decay_log, skip_gain, step_bias = head_terms
    pieces = projected.shape[0]
    span_count = pieces // SPAN
    stream = stream_in.astype(jnp.float32)
    inv_rms = lax.rsqrt(jnp.mean(stream * stream, axis=-1, keepdims=True) + epsilon)
    padded, conv_pre, values, inputs_b, readout, step_pre, step_size, step_spans, cumul = prepare(
        projected, edge, conv_full, bias_full, decay_log, step_bias
    )
    scores = jnp.einsum("ctn,csn->cts", readout, inputs_b, precision=highest)
    decay_mat, step_heads, weights = block_terms(cumul, step_spans, scores)
    expo_tail = jnp.exp(cumul[:, -1:, :] - cumul)
    tail_w = expo_tail * step_spans
    span_decay = jnp.exp(cumul[:, -1, :])
    growth = jnp.exp(cumul)
    inter_out = growth[..., None] * jnp.einsum("ctn,chpn->cthp", readout, starts, precision=highest)
    gate_raw = projected[:, :INNER].astype(jnp.float32)
    gate_act = jax.nn.silu(gate_raw)
    gate_val = mixed_out * gate_act
    gate_rms = lax.rsqrt(jnp.mean(gate_val * gate_val, axis=-1, keepdims=True) + epsilon)
    gated = (gate_val * gate_rms * gain_full.astype(jnp.float32)).astype(jnp.bfloat16)
    out_grad = jnp.dot(gated.T, cotan, preferred_element_type=jnp.float32)
    d_gated = jnp.dot(cotan, out_full.T, preferred_element_type=jnp.float32)
    gain_grad = jnp.sum(d_gated * gate_val * gate_rms, axis=0)
    d_hat = d_gated * gain_full.astype(jnp.float32)
    d_gate = gate_rms * d_hat - gate_val * gate_rms**3 * jnp.mean(
        d_hat * gate_val, axis=-1, keepdims=True
    )
    d_gate_raw = d_gate * mixed_out * silu_grad(gate_raw)
    d_mixed = (d_gate * gate_act).reshape(span_count, SPAN, HEADS, HEADDIM)
    skip_grad = jnp.sum(d_mixed * values, axis=(0, 1, 3))
    d_values = skip_gain[:, None] * d_mixed
    scaled = growth[..., None] * d_mixed
    d_start = jnp.einsum("cthp,ctn->chpn", scaled, readout, precision=highest)
    d_readout = jnp.einsum("cthp,chpn->ctn", scaled, starts, precision=highest)
    d_cumul = jnp.sum(d_mixed * inter_out, axis=-1)
    ones_heads = jnp.ones((HEADS,), jnp.float32)
    zero_state = jnp.zeros((HEADS, HEADDIM, NSTATE), jnp.float32)
    lead_grad, _ = lax.scan(retreat, zero_state, (span_decay, d_start), reverse=True)
    arriving = carried_in((piece_decay, lead_grad), "ctx", combine, (ones_heads, zero_state), True)[
        1
    ]
    _, d_after = lax.scan(retreat, arriving, (span_decay, d_start), reverse=True)
    d_decay = jnp.sum(d_after * starts, axis=(2, 3))
    proj_state = jnp.einsum("chpn,csn->cshp", d_after, inputs_b, precision=highest)
    d_values = d_values + tail_w[..., None] * proj_state
    d_inputs_b = jnp.einsum(
        "cshp,chpn->csn", tail_w[..., None] * values, d_after, precision=highest
    )
    d_tail = jnp.sum(values * proj_state, axis=-1)
    tail_term = d_tail * tail_w
    d_step = d_tail * expo_tail
    end_grad = d_decay * span_decay + jnp.sum(tail_term, axis=1)
    d_cumul = d_cumul - tail_term
    d_weights = jnp.einsum("cthp,cshp->chts", d_mixed, values, precision=highest)
    d_values = d_values + jnp.einsum("chts,cthp->cshp", weights, d_mixed, precision=highest)
    weighted = d_weights * weights
    d_cumul = d_cumul + jnp.swapaxes(jnp.sum(weighted, axis=3) - jnp.sum(weighted, axis=2), 1, 2)
    d_scores = jnp.sum(d_weights * decay_mat * step_heads[:, :, None, :], axis=1)
    d_step = d_step + jnp.swapaxes(jnp.sum(d_weights * scores[:, None] * decay_mat, axis=2), 1, 2)
    d_readout = d_readout + jnp.einsum("cts,csn->ctn", d_scores, inputs_b, precision=highest)
    d_inputs_b = d_inputs_b + jnp.einsum("cts,ctn->csn", d_scores, readout, precision=highest)
    d_cumul = d_cumul.at[:, -1, :].add(end_grad)
    d_log = jnp.flip(jnp.cumsum(jnp.flip(d_cumul, 1), axis=1), 1).reshape(pieces, HEADS)
    rate_head = -jnp.exp(decay_log)
    decay_log_grad = jnp.sum(d_log * step_size, axis=0) * rate_head
    d_step_pre = (d_step.reshape(pieces, HEADS) + d_log * rate_head) * jax.nn.sigmoid(step_pre)
    step_bias_grad = jnp.sum(d_step_pre, axis=0)
    d_active = jnp.concatenate(
        [
            d_values.reshape(pieces, INNER),
            d_inputs_b.reshape(pieces, NSTATE),
            d_readout.reshape(pieces, NSTATE),
        ],
        axis=1,
    )
    d_conv = d_active * silu_grad(conv_pre)
    bias_grad = jnp.sum(d_conv, axis=0)
    conv_grad = jnp.stack(
        [jnp.sum(d_conv * padded[offset : offset + pieces], axis=0) for offset in range(CONV)]
    )
    conv_taps = conv_full.astype(jnp.float32)
    d_padded = sum(
        (
            jnp.pad(d_conv * conv_taps[offset], ((offset, CONV - 1 - offset), (0, 0)))
            for offset in range(CONV)
        )
    )
    back_edge = passed_along(d_padded[: CONV - 1], "ctx", -1)
    d_conv_in = d_padded[CONV - 1 :] + jnp.pad(back_edge, ((pieces - CONV + 1, 0), (0, 0)))
    d_projected = jnp.concatenate([d_gate_raw, d_conv_in, d_step_pre], axis=1).astype(jnp.bfloat16)
    in_grad = jnp.dot(normed.T, d_projected, preferred_element_type=jnp.float32)
    d_normed = jnp.dot(d_projected, in_full.T, preferred_element_type=jnp.float32)
    norm_grad = jnp.sum(d_normed * stream * inv_rms, axis=0)
    d_hat_in = d_normed * norm_full.astype(jnp.float32)
    d_stream = inv_rms * d_hat_in - stream * inv_rms**3 * jnp.mean(
        d_hat_in * stream, axis=-1, keepdims=True
    )
    input_grad = (cotan.astype(jnp.float32) + d_stream).astype(jnp.bfloat16)
    return (
        input_grad,
        (norm_grad, in_grad, conv_grad, bias_grad, gain_grad, out_grad),
        (decay_log_grad, skip_grad, step_bias_grad),
    )


def on_device(
    tokens,
    norm_weight,
    in_weight,
    conv_weight,
    conv_bias,
    decay_log,
    skip_gain,
    step_bias,
    gated_gain,
    out_weight,
    cotangent,
):
    head_terms = (decay_log, skip_gain, step_bias)
    held = (
        lax.all_gather(norm_weight, "dp", axis=0, tiled=True),
        lax.all_gather(in_weight, "dp", axis=0, tiled=True),
        lax.all_gather(conv_weight, "dp", axis=1, tiled=True),
        lax.all_gather(conv_bias, "dp", axis=0, tiled=True),
        lax.all_gather(gated_gain, "dp", axis=0, tiled=True),
        lax.all_gather(out_weight, "dp", axis=0, tiled=True),
    )
    results = []
    saved = []
    for micro_index in range(MICRO):
        result, stored = forward(tokens[micro_index], held, head_terms)
        results.append(result)
        saved.append(stored)
    input_grads = [None] * MICRO
    totals = None
    head_totals = None
    for micro_index in reversed(range(MICRO)):
        input_grad, owned_part, head_part = backward(
            tokens[micro_index], saved[micro_index], cotangent[micro_index], held, head_terms
        )
        input_grads[micro_index] = input_grad
        if micro_index == MICRO - 1:
            totals, head_totals = (owned_part, head_part)
        else:
            totals = tuple((running + addend for running, addend in zip(totals, owned_part)))
            head_totals = tuple(
                (running + addend for running, addend in zip(head_totals, head_part))
            )
    owned = (
        lax.psum_scatter(totals[0], "dp", scatter_dimension=0, tiled=True),
        lax.psum_scatter(totals[1], "dp", scatter_dimension=0, tiled=True),
        lax.psum_scatter(totals[2], "dp", scatter_dimension=1, tiled=True),
        lax.psum_scatter(totals[3], "dp", scatter_dimension=0, tiled=True),
        lax.psum_scatter(totals[4], "dp", scatter_dimension=0, tiled=True),
        lax.psum_scatter(totals[5], "dp", scatter_dimension=0, tiled=True),
    )
    owned = lax.psum(owned, "ctx")
    head_sums = lax.psum(head_totals, ("dp", "ctx"))
    return (
        jnp.stack(results),
        jnp.stack(input_grads),
        owned[0],
        owned[1],
        owned[2],
        owned[3],
        head_sums[0],
        head_sums[1],
        head_sums[2],
        owned[4],
        owned[5],
    )


def solution(mesh):
    return jax.shard_map(
        on_device,
        mesh=mesh,
        in_specs=(
            P("dp", "ctx", None),
            P("dp"),
            P("dp", None),
            P(None, "dp"),
            P("dp"),
            P(),
            P(),
            P(),
            P("dp"),
            P("dp", None),
            P("dp", "ctx", None),
        ),
        out_specs=(
            P("dp", "ctx", None),
            P("dp", "ctx", None),
            P("dp"),
            P("dp", None),
            P(None, "dp"),
            P("dp"),
            P(),
            P(),
            P(),
            P("dp"),
            P("dp", None),
        ),
        check_vma=False,
    )
```

profile of v0, /device:TPU:0, one launch (start us, length us, event | category | flops | bytes accessed | tf_op | source)
XLA Modules:
  0.0 767.3 jit_solution(3655112943691557882)
XLA Ops:
  13.8 39.6 %all-reduce.23 = (bf16[768]{0:T(1024)(128)(2,1)S(1)}, bf16[1792]{0:T(1024)(128)(2,1)S(1)}, bf16[1536]{0:T(1024)(128)(2,1)}) all-reduce(bf16[768]{0:T(1024)(128)(2,1)S(1)} %dynamic-update-slice.7, bf16[1792]{0:T(1024)(128)(2,1)S(1)} %dynamic-update-slice.6, bf16[1536]{0:T(1024)(128)(2,1)S(1)} %dynamic-update-slice.9), channel_id=1, replica_groups=mesh['dp'=8,'ctx'=4] {'dp'}, use_global_device_ids=true, to_apply=%add.11 | all-reduce | flops 4096 | bytes 16384
  54.1 26.8 %all-gather.6 = bf16[8,224,4]{1,2,0:T(4,128)(2,1)S(1)} all-gather(bf16[1,224,4]{1,2,0:T(4,128)(2,1)} %bitcast.390), channel_id=1, replica_groups=mesh['dp'=8,'ctx'=4] {'dp'}, dimensions={0}, use_global_device_ids=true | all-gather | bytes 16128 | tf_op jit(solution)/shard_map/all_gather | solution.py:260
  83.6 17.2 %all-gather.14.cloned.1.call-done = bf16[768,3352]{1,0:T(8,128)(2,1)} async-done(((bf16[96,3352]{1,0:T(8,128)(2,1)}), bf16[768,3352]{1,0:T(8,128)(2,1)}) %all-gather.14.cloned.1.call-update) | async-done | bytes 5148688 | tf_op jit(solution)/shard_map/all_gather | solution.py:259
  100.8 4.9 convolution_convert_fusion
  113.4 4.5 collective-permute-start
  119.7 5.6 fusion.19
  133.9 4.1 fusion.68
  138.0 3.9 while.175
  160.9 4.1 fusion.72
  165.0 3.8 while.174
  186.0 12.2 %all-reduce.21 = (f32[96]{0:T(128)S(1)}, f32[96]{0:T(128)}) all-reduce(f32[96]{0:T(128)S(1)} %dynamic-update-slice.10, f32[96]{0:T(128)S(1)} %dynamic-update-slice.8), channel_id=5, replica_groups=mesh['dp'=8,'ctx'=4] {'ctx'}, use_global_device_ids=true, to_apply=%add.14 | all-reduce | flops 192 | bytes 1536
  206.1 3.8 while.169
  214.2 6.3 bitcast_add_fusion.16
  224.5 3.8 while.167
  232.5 6.2 bitcast_add_fusion.17
  244.1 16.8 %all-gather.16.cloned.1.call-done = bf16[1536,768]{1,0:T(8,128)(2,1)} async-done(((bf16[192,768]{1,0:T(8,128)(2,1)}), bf16[1536,768]{1,0:T(8,128)(2,1)}) %all-gather.16.cloned.1.call-update) | async-done | bytes 2359312 | tf_op jit(solution)/shard_map/all_gather | solution.py:263
  261.0 3.8 multiply_reduce_fusion.13
  265.5 5.7 multiply_reduce_fusion.15
  274.4 4.2 fusion.60
  278.6 4.9 while.177
  285.1 5.6 multiply_reduce_fusion.14
  293.8 4.1 fusion.64
  297.9 4.8 while.176
  306.3 4.7 fusion.102
  311.1 5.4 fusion.79
  316.6 11.1 %fusion.12 = (f32[2,24,128]{2,1,0:T(8,128)}, f32[2,24,128]{2,1,0:T(8,128)}, f32[2,24,128]{2,1,0:T(8,128)}, f32[2,128,128]{2,1,0:T(8,128)S(1)}, f32[2,128,128]{2,...) fusion(f32[2,24,128]{2,1,0:T(8,128)S(1)} %copy-done.149, ...), kind=kOutput, calls=%fused_computation.66 | convolution fusion | flops 624324608 | bytes 7077888 | tf_op jit(solution)/shard_map/cthp,cshp->chts/dot_general | solution.py:191
  328.7 4.6 fusion.105
  343.5 6.1 while.172
  351.0 3.8 while.173
  357.7 3.7 multiply_reduce_fusion.18
  363.8 6.1 while.170
  371.4 4.1 while.171
  378.0 4.6 multiply_reduce_fusion.22
  383.8 6.1 bitcast_add_fusion.15
  396.9 6.4 bitcast_add_fusion.14
  410.2 8.5 %multiply_reduce_fusion.7 = (f32[1792]{0:T(1024)S(1)}, f32[1792]{0:T(1024)S(1)}, f32[1792]{0:T(1024)S(1)}, f32[1792]{0:T(1024)S(1)}, f32[1792]{0:T(1024)S(1)}, /*index=5*/f32[256,1792]{0,1:T(8,128)S(1)}) fusion(f32[259,1792]{0,1:T(8,128)} %copy-done, f32[256,1792]{0,1:T(8,128)} %get-tuple-element.1047, f32[256,128]{0,1:T(8,128)S(1)} %copy-done.84, ...), kind=kLoop, calls=%fused_computation.79 | loop fusion | flops 8707328 | bytes 12880896 | tf_op jit(solution)/shard_map/reduce_sum | solution.py:216
  422.2 3.5 broadcast_multiply_fusion.6
  435.2 6.9 pad_add_fusion
  442.2 3.8 pad_add_fusion.1
  453.3 5.8 convolution_add_fusion
  468.4 45.6 %all-reduce.18 = (f32[24]{0:T(128)}, f32[24]{0:T(128)}, f32[24]{0:T(128)}) all-reduce(f32[24]{0:T(128)S(1)} %add_multiply_fusion, f32[24]{0:T(128)S(1)} %add.621, f32[24]{0:T(128)S(1)} %add.622), channel_id=1, replica_groups=mesh['dp'=8,'ctx'=4] {'dp','ctx'}, use_global_device_ids=true, to_apply=%region_74.75 | all-reduce | flops 72 | bytes 576 | tf_op jit(solution)/shard_map/psum | solution.py:295
  514.1 5.1 fusion.140
  519.2 121.9 %reduce-scatter.6.cloned.1.call-done = f32[96,3352]{1,0:T(8,128)} async-done(((f32[768,3352]{1,0:T(8,128)}), f32[96,3352]{1,0:T(8,128)}) %reduce-scatter.6.cloned.1.call-update) | async-done | bytes 1287184 | tf_op jit(solution)/shard_map/reduce_scatter | solution.py:288
  641.2 5.4 fusion.127
  646.6 35.4 %all-reduce.19 = (f32[768]{0:T(1024)S(1)}, f32[1792]{0:T(1024)S(1)}, f32[1536]{0:T(1024)S(1)}) all-reduce(f32[768]{0:T(1024)S(1)} %add.616, f32[1792]{0:T(1024)S(1)} %add.619, f32[1536]{0:T(1024)S(1)} %add.623), channel_id=8, replica_groups=mesh['dp'=8,'ctx'=4] {'dp'}, use_global_device_ids=true, to_apply=%region_54.55.clone | all-reduce | flops 4096 | bytes 32768
  685.0 21.8 %reduce-scatter.10.cloned.1.call-done = f32[224,4]{1,0:T(8,128)} async-done(((f32[1792,4]{1,0:T(8,128)}), f32[224,4]{1,0:T(8,128)}) %reduce-scatter.10.cloned.1.call-update) | async-done | bytes 3600
  707.8 6.3 all-reduce.20
  714.1 42.8 %all-reduce.26.cloned.1.call-done = (f32[96,3352]{1,0:T(8,128)}, f32[192,768]{1,0:T(8,128)}) async-done(((f32[96,3352]{1,0:T(8,128)}, f32[192,768]{1,0:T(8,128)}), (f32[96,3352]{1,0:T(8,128)}, f32[192,768]{1,0:T(8,128)})) %all-reduce.26.cloned.1.call-update) | async-done | bytes 1877008 | tf_op jit(solution)/shard_map/psum | solution.py:294
  (651 shorter events, 213.9 us)
Async XLA Ops:
  7.2 93.7 %copy-start.42 = (bf16[2,256,768]{2,1,0:T(8,128)(2,1)S(1)}, bf16[2,256,768]{2,1,0:T(8,128)(2,1)}, u32[]{:S(2)}) copy-start(bf16[2,256,768]{2,1,0:T(8,128)(2,1)} %param.39) | copy-start | bytes 2359300
  7.2 75.8 %copy-start.176 = (f32[24]{0:T(128)S(1)}, f32[24]{0:T(128)}, u32[]{:S(2)}) copy-start(f32[24]{0:T(128)} %param.44) | copy-start | bytes 292
  7.2 93.6 %all-gather.14.cloned.1.call-start = ((), (), s32[]{:S(2)}) async-start(), calls=%async_computation.3 | async-start | bytes 5971968 | tf_op jit(solution)/shard_map/all_gather | solution.py:259
  7.9 196.2 %all-gather.20.cloned.1.call-start = ((), (), s32[]{:S(2)}) async-start(), calls=%async_computation.8 | async-start | bytes 3932160 | tf_op jit(solution)/shard_map/all_gather | solution.py:30
  53.5 52.3 %copy-start.81 = (f32[768]{0:T(1024)}, f32[768]{0:T(1024)S(1)}, u32[]{:S(2)}) copy-start(f32[768]{0:T(1024)S(1)} %convert_element_type.124) | copy-start | bytes 9220
  81.6 38.0 %copy-start.110 = (f32[1792]{0:T(1024)}, f32[1792]{0:T(1024)S(1)}, u32[]{:S(2)}) copy-start(f32[1792]{0:T(1024)S(1)} %get-tuple-element.886) | copy-start | bytes 21508
  83.0 25.1 %copy-start.172 = (f32[24]{0:T(128)}, f32[24]{0:T(128)S(1)}, u32[]{:S(2)}) copy-start(f32[24]{0:T(128)S(1)} %exponential_negate_fusion) | copy-start | bytes 292
  83.6 22.1 %copy-start.124 = (f32[256]{0:T(256)}, f32[256]{0:T(256)S(1)}, u32[]{:S(2)}) copy-start(f32[256]{0:T(256)S(1)} %get-tuple-element.1098) | copy-start | bytes 3076
  83.6 22.2 %copy-start.151 = (f32[256]{0:T(256)}, f32[256]{0:T(256)S(1)}, u32[]{:S(2)}) copy-start(f32[256]{0:T(256)S(1)} %get-tuple-element.1112) | copy-start | bytes 3076
  110.6 7.3 collective-permute-start.1
  113.4 5.6 collective-permute-start
  141.9 11.1 %copy-start.158 = (f32[24]{0:T(128)}, f32[24]{0:T(128)S(1)}, u32[]{:S(2)}) copy-start(f32[24]{0:T(128)S(1)} %get-tuple-element.780) | copy-start | bytes 292
  142.8 80.1 %all-gather.18.cloned.1.call-start = ((), (), s32[]{:S(2)}) async-start(), calls=%async_computation.7 | async-start | bytes 3932160 | tf_op jit(solution)/shard_map/all_gather | solution.py:30
  169.7 14.5 %copy-start.76 = (f32[2,128,128]{1,0,2:T(2,128)S(1)}, f32[2,128,128]{1,0,2:T(2,128)}, u32[]{:S(2)}) copy-start(f32[2,128,128]{1,0,2:T(2,128)} %reshape.320) | copy-start | bytes 393220
  169.7 14.6 %copy-start.77 = (f32[2,128,128]{1,0,2:T(2,128)S(1)}, f32[2,128,128]{1,0,2:T(2,128)}, u32[]{:S(2)}) copy-start(f32[2,128,128]{1,0,2:T(2,128)} %reshape.314) | copy-start | bytes 393220
  169.7 29.1 %copy-start.85 = (f32[256,128]{0,1:T(8,128)S(1)}, f32[256,128]{0,1:T(8,128)}, u32[]{:S(2)}) copy-start(f32[256,128]{0,1:T(8,128)} %get-tuple-element.1063) | copy-start | bytes 393220
  169.7 31.3 %copy-start.86 = (f32[256,128]{0,1:T(8,128)S(1)}, f32[256,128]{0,1:T(8,128)}, u32[]{:S(2)}) copy-start(f32[256,128]{0,1:T(8,128)} %get-tuple-element.1060) | copy-start | bytes 393220
  169.8 91.2 %all-gather.16.cloned.1.call-start = ((), (), s32[]{:S(2)}) async-start(), calls=%async_computation.4 | async-start | bytes 2654208 | tf_op jit(solution)/shard_map/all_gather | solution.py:263
  170.3 173.1 %all-gather.24.cloned.1.call-start = ((), (), s32[]{:S(2)}) async-start(), calls=%async_computation.10 | async-start | bytes 3932160 | tf_op jit(solution)/shard_map/all_gather | solution.py:30
  184.3 19.8 %copy-start.72 = (f32[2,128,128]{2,1,0:T(8,128)}, f32[2,128,128]{2,1,0:T(8,128)S(1)}, u32[]{:S(2)}) copy-start(f32[2,128,128]{2,1,0:T(8,128)S(1)} %copy.429) | copy-start | bytes 393220
  184.4 19.7 %copy-start.74 = (f32[2,128,128]{2,1,0:T(8,128)}, f32[2,128,128]{2,1,0:T(8,128)S(1)}, u32[]{:S(2)}) copy-start(f32[2,128,128]{2,1,0:T(8,128)S(1)} %copy.414) | copy-start | bytes 393220
  232.5 7.5 copy-start.40
  232.5 7.5 copy-start.49
  232.5 7.5 copy-start.52
  232.5 7.5 copy-start.62
  240.2 20.7 %copy-start.54 = (bf16[2,256,768]{2,1,0:T(8,128)(2,1)S(1)}, bf16[2,256,768]{2,1,0:T(8,128)(2,1)}, u32[]{:S(2)}) copy-start(bf16[2,256,768]{2,1,0:T(8,128)(2,1)} %param.49) | copy-start | bytes 2359300
  284.3 79.4 %all-gather.22.cloned.1.call-start = ((), (), s32[]{:S(2)}) async-start(), calls=%async_computation.9 | async-start | bytes 3932160 | tf_op jit(solution)/shard_map/all_gather | solution.py:30
  303.6 215.6 %reduce-scatter.8.cloned.1.call-start = ((), (), s32[]{:S(2)}) async-start(), calls=%async_computation.6 | async-start | bytes 5308416 | tf_op jit(solution)/shard_map/reduce_scatter | solution.py:292
  316.6 11.1 %copy-start.75 = (f32[2,128,128]{2,1,0:T(8,128)S(1)}, f32[2,128,128]{2,1,0:T(8,128)}, u32[]{:S(2)}) copy-start(f32[2,128,128]{2,1,0:T(8,128)} %copy-done.74) | copy-start | bytes 393220
  316.6 12.1 %copy-start.91 = (f32[2,128,24]{1,2,0:T(8,128)S(1)}, f32[2,128,24]{1,2,0:T(8,128)}, u32[]{:S(2)}) copy-start(f32[2,128,24]{1,2,0:T(8,128)} %copy.435) | copy-start | bytes 73732
  343.4 297.7 %reduce-scatter.6.cloned.1.call-start = ((), (), s32[]{:S(2)}) async-start(), calls=%async_computation.5 | async-start | bytes 11943936 | tf_op jit(solution)/shard_map/reduce_scatter | solution.py:288
  410.2 8.6 %copy-start.45 = (f32[256,1792]{0,1:T(8,128)S(1)}, f32[256,1792]{0,1:T(8,128)}, u32[]{:S(2)}) copy-start(f32[256,1792]{0,1:T(8,128)} %get-tuple-element.1081) | copy-start | bytes 5505028
  410.2 8.6 %copy-start.50 = (f32[192,8,2,128]{3,1,2,0:T(8,128)S(1)}, f32[192,8,2,128]{3,1,2,0:T(8,128)}, u32[]{:S(2)}) copy-start(f32[192,8,2,128]{3,1,2,0:T(8,128)} %copy.630) | copy-start | bytes 4718596
  410.2 8.6 %copy-start.83 = (f32[256,128]{0,1:T(8,128)S(1)}, f32[256,128]{0,1:T(8,128)}, u32[]{:S(2)}) copy-start(f32[256,128]{0,1:T(8,128)} %copy.531) | copy-start | bytes 393220
  429.6 16.7 %collective-permute-start.3 = (f32[3,1792]{1,0:T(4,128)S(1)}, f32[3,1792]{1,0:T(4,128)S(1)}, u32[]{:S(2)}, u32[]{:S(2)}) collective-permute-start(f32[3,1792]{1,0:T(4,128)S(1)} %copy.481), channel_id=1, source_target_pairs={{1,0},{2,1},{3,2},{5,4},{6,5},{7,6},{9,8},{10,9},{11,10},{13,12},{... | collective-permute-start | bytes 64520 | tf_op jit(solution)/shard_map/ppermute | solution.py:23
  433.3 8.9 %copy-start.32 = (f32[256,1792]{0,1:T(8,128)S(1)}, f32[256,1792]{0,1:T(8,128)}, u32[]{:S(2)}) copy-start(f32[256,1792]{0,1:T(8,128)} %get-tuple-element.1083) | copy-start | bytes 5505028
  433.3 8.9 %copy-start.33 = (f32[256,1792]{0,1:T(8,128)S(1)}, f32[256,1792]{0,1:T(8,128)}, u32[]{:S(2)}) copy-start(f32[256,1792]{0,1:T(8,128)} %get-tuple-element.1084) | copy-start | bytes 5505028
  433.3 8.9 %copy-start.34 = (f32[256,1792]{0,1:T(8,128)S(1)}, f32[256,1792]{0,1:T(8,128)}, u32[]{:S(2)}) copy-start(f32[256,1792]{0,1:T(8,128)} %get-tuple-element.1085) | copy-start | bytes 5505028
  433.3 13.4 %collective-permute-start.2 = (f32[3,1792]{1,0:T(4,128)S(1)}, f32[3,1792]{1,0:T(4,128)S(1)}, u32[]{:S(2)}, u32[]{:S(2)}) collective-permute-start(f32[3,1792]{1,0:T(4,128)S(1)} %copy.457), channel_id=1, source_target_pairs={{1,0},{2,1},{3,2},{5,4},{6,5},{7,6},{9,8},{10,9},{11,10},{13,12},{... | collective-permute-start | bytes 64520 | tf_op jit(solution)/shard_map/ppermute | solution.py:23
  459.2 247.6 %reduce-scatter.10.cloned.1.call-start = ((), (), s32[]{:S(2)}) async-start(), calls=%async_computation.11 | async-start | bytes 1032192
  465.9 48.2 %copy-start.60 = (bf16[256,1792]{0,1:T(8,128)(2,1)S(1)}, bf16[256,1792]{0,1:T(8,128)(2,1)}, u32[]{:S(2)}) copy-start(bf16[256,1792]{0,1:T(8,128)(2,1)} %copy-done.59) | copy-start | bytes 2752516
  465.9 48.2 %copy-start.65 = (bf16[256,1536]{0,1:T(8,128)(2,1)S(1)}, bf16[256,1536]{0,1:T(8,128)(2,1)}, u32[]{:S(2)}) copy-start(bf16[256,1536]{0,1:T(8,128)(2,1)} %get-tuple-element.1050) | copy-start | bytes 2359300
  468.4 288.6 %all-reduce.26.cloned.1.call-start = ((), (), s32[]{:S(2)}) async-start(), calls=%async_computation.12 | async-start | bytes 3833856 | tf_op jit(solution)/shard_map/psum | solution.py:294
  519.2 121.9 %copy-start.58 = (bf16[256,1792]{0,1:T(8,128)(2,1)S(1)}, bf16[256,1792]{0,1:T(8,128)(2,1)}, u32[]{:S(2)}) copy-start(bf16[256,1792]{0,1:T(8,128)(2,1)} %copy-done.57) | copy-start | bytes 2752516
  519.2 121.9 %copy-start.78 = (f32[256,768]{1,0:T(8,128)S(1)}, f32[256,768]{1,0:T(8,128)}, u32[]{:S(2)}) copy-start(f32[256,768]{1,0:T(8,128)} %fusion.140) | copy-start | bytes 2359300
  641.1 41.1 %copy-start.56 = (bf16[2,256,768]{2,1,0:T(8,128)(2,1)S(1)}, bf16[2,256,768]{2,1,0:T(8,128)(2,1)}, u32[]{:S(2)}) copy-start(bf16[2,256,768]{2,1,0:T(8,128)(2,1)} %param.49) | copy-start | bytes 2359300
  641.1 41.1 %copy-start.167 = (f32[256]{0:T(256)S(1)}, f32[256]{0:T(256)}, u32[]{:S(2)}) copy-start(f32[256]{0:T(256)} %get-tuple-element.1097) | copy-start | bytes 3076
  641.2 41.1 %copy-start.168 = (f32[256]{0:T(256)S(1)}, f32[256]{0:T(256)}, u32[]{:S(2)}) copy-start(f32[256]{0:T(256)} %get-tuple-element.1113) | copy-start | bytes 3076
  (155 other events, 510.1 us)
Sparse Core Ops, SparseCore 0:
  10.2 90.5 all-gather.13
  142.9 33.0 all-gather.19
  178.1 28.6 all-gather.17
  208.8 52.0 all-gather.15
  284.5 27.0 all-gather.23
  313.6 28.5 all-gather.21
  345.8 95.3 reduce-scatter.7
  459.3 181.7 reduce-scatter.5
  644.8 62.0 reduce-scatter.9
  709.1 47.7 all-reduce.25
where the time goes:
time: 775 us; the launch traced here: 767 us
  waiting for transfers between devices  222 us (29%)
  blocking collectives  166 us (21%)
  matrix products  133 us (17%)
  local copies, waits for them, and re-layouts  119 us (15%)
  other arithmetic  94.4 us (12%)
  between operations  21.6 us (3%)
  starting transfers between devices  9.65 us (1%)
    reduce_scatter x1, waiting for transfers between devices, on_device(): lax.psum_scatter(totals[1], 'dp', scatter_dimension=0, tiled=True)  122 us
    unnamed x3, blocking collectives  87.1 us
    psum x1, blocking collectives, on_device(): head_sums = lax.psum(head_totals, ('dp', 'ctx'))  45.6 us
    psum x1, waiting for transfers between devices, on_device(): owned = lax.psum(owned, 'ctx')  42.8 us
    unnamed x363, local copies, waits for them, and re-layouts  30.6 us
    all_gather x1, blocking collectives, on_device(): lax.all_gather(conv_weight, 'dp', axis=1, tiled=True)  26.8 us
    unnamed x11, waiting for transfers between devices  23.1 us
    all_gather x1, waiting for transfers between devices, on_device(): lax.all_gather(in_weight, 'dp', axis=0, tiled=True)  17.2 us
  transfers between devices with their start and end apart: 14, of which 6 were waited for; matrix products, arithmetic and copies ran while one was open for 35% of the time, Pallas kernels for 0%

commit v1 on v0

v1 whole, which is shorter than its diff:
```python
import jax
import jax.numpy as jnp
from jax import lax
from jax.experimental import pallas as pl
from jax.experimental.pallas import tpu as pltpu
from jax.sharding import PartitionSpec as P

HEADS = 24
HEADDIM = 64
NSTATE = 128
CONV = 4
SPAN = 128
INNER = 1536
XBC = 1792
WIDE = 1920
SPARE = 104
PAIRS = HEADS // 2
TAIL_ROWS = 16

epsilon = 1e-05
low = jnp.bfloat16
f32 = jnp.float32


def nn(a, b, precision=None):
    return lax.dot_general(
        a, b, (((1,), (0,)), ((), ())), precision=precision, preferred_element_type=f32
    )


def nt(a, b):
    return lax.dot_general(a, b, (((1,), (1,)), ((), ())), preferred_element_type=f32)


def tn(a, b):
    return lax.dot_general(a, b, (((0,), (0,)), ((), ())), preferred_element_type=f32)


def silu_grad(pre):
    sigma = jax.nn.sigmoid(pre)
    return sigma * (1.0 + pre * (1.0 - sigma))


def first_half(rows):
    return lax.broadcasted_iota(jnp.int32, (rows, SPAN), 1) < HEADDIM


def expand(per_head):
    rows = per_head.shape[0]
    mask = first_half(rows)
    pieces = []
    for pair in range(PAIRS):
        left = jnp.broadcast_to(per_head[:, 2 * pair : 2 * pair + 1], (rows, SPAN))
        right = jnp.broadcast_to(per_head[:, 2 * pair + 1 : 2 * pair + 2], (rows, SPAN))
        pieces.append(jnp.where(mask, left, right))
    return jnp.concatenate(pieces, axis=1)


def head_sum(wide, fold):
    high = wide.astype(low)
    rest = (wide - high.astype(f32)).astype(low)
    return nn(high, fold) + nn(rest, fold)


def diagonal(block, mask):
    zero = jnp.zeros_like(block)
    return jnp.concatenate(
        [jnp.where(mask, block, zero), jnp.where(mask, zero, block)], axis=0
    ).astype(low)


def causal_mask():
    row = lax.broadcasted_iota(jnp.int32, (SPAN, SPAN), 0)
    column = lax.broadcasted_iota(jnp.int32, (SPAN, SPAN), 1)
    return row >= column


def decay_of(cumul, cumul_t, head, causal):
    gap = cumul[:, head : head + 1] - cumul_t[head : head + 1, :]
    return jnp.exp(jnp.where(causal, gap, -1e30))


def prepare_kernel(
    cs_ref, halo_ref, taps_ref, bias_ref, head_ref,
    pre_ref, cumul_ref, cumul_t_ref, step_ref, step_t_ref, sigma_ref, update_ref, decay_ref,
    padded,
):
    padded[0:8, :] = halo_ref[0]
    padded[8:, :] = cs_ref[:, :XBC].astype(f32)
    pre = bias_ref[...] + sum(
        padded[5 + k : 5 + k + SPAN, :] * taps_ref[k : k + 1, :] for k in range(CONV)
    )
    pre_ref[...] = pre
    active = pre * jax.nn.sigmoid(pre)
    values = active[:, :INNER]
    inputs_b = active[:, INNER : INNER + NSTATE].astype(low)
    lane = lax.broadcasted_iota(jnp.int32, (SPAN, SPAN), 1)
    raw = jnp.where(lane < HEADS, cs_ref[:, XBC:].astype(f32) + head_ref[0:1, :], 0.0)
    step = jnp.maximum(raw, 0.0) + jnp.log1p(jnp.exp(-jnp.abs(raw)))
    step = jnp.where(lane < HEADS, step, 0.0)
    sigma_ref[...] = jax.nn.sigmoid(raw)
    log_step = step * (-jnp.exp(head_ref[1:2, :]))
    lower = causal_mask().astype(f32)
    cumul = nn(lower, log_step, lax.Precision.HIGHEST)
    cumul_ref[...] = cumul
    step_ref[...] = step
    cumul_t_ref[...] = cumul.T
    step_t_ref[...] = step.T
    last = cumul[SPAN - 1 : SPAN, :]
    tail = jnp.exp(last - cumul) * step
    update_ref[0] = tn(inputs_b, (expand(tail) * values).astype(low))
    decay_ref[0] = jnp.broadcast_to(expand(jnp.exp(last)), (8, INNER))


def intra_kernel(pre_ref, cumul_ref, cumul_t_ref, step_t_ref, skip_ref, out_ref):
    pre = pre_ref[...]
    active = pre * jax.nn.sigmoid(pre)
    inputs_b = active[:, INNER : INNER + NSTATE].astype(low)
    readout = active[:, INNER + NSTATE :].astype(low)
    scores = nt(readout, inputs_b)
    causal = causal_mask()
    mask = first_half(SPAN)
    cumul, cumul_t, step_t = cumul_ref[...], cumul_t_ref[...], step_t_ref[...]
    for pair in range(PAIRS):
        cut = slice(pair * SPAN, (pair + 1) * SPAN)
        values = active[:, cut]
        weights = [
            (scores * decay_of(cumul, cumul_t, h, causal) * step_t[h : h + 1, :]).astype(low)
            for h in (2 * pair, 2 * pair + 1)
        ]
        inner = nn(jnp.concatenate(weights, axis=1), diagonal(values, mask))
        out_ref[:, cut] = inner + skip_ref[:, cut] * values


def gate_kernel(
    partial_ref, pre_ref, cumul_ref, start_ref, gate_ref, dgated_ref, gain_ref, fold_ref,
    gated_ref, dgate_ref, dmixed_ref, dstart_ref, dcumul_ref, sums_ref,
):
    @pl.when((pl.program_id(0) == 0) & (pl.program_id(1) == 0))
    def _():
        sums_ref[...] = jnp.zeros_like(sums_ref)

    pre = pre_ref[...]
    active = pre * jax.nn.sigmoid(pre)
    values = active[:, :INNER]
    readout = active[:, INNER + NSTATE :].astype(low)
    growth = expand(jnp.exp(cumul_ref[...]))
    inter = growth * nn(readout, start_ref[0].astype(low))
    mixed = partial_ref[...] + inter
    gate = gate_ref[...].astype(f32)
    sigma = jax.nn.sigmoid(gate)
    act = gate * sigma
    gate_val = mixed * act
    rms = lax.rsqrt(jnp.mean(gate_val * gate_val, axis=1, keepdims=True) + epsilon)
    hat = gate_val * rms
    gain = gain_ref[...]
    gated_ref[...] = (hat * gain).astype(low)
    d_gated = dgated_ref[...]
    sums_ref[0:1, :] += jnp.sum(d_gated * hat, axis=0, keepdims=True)
    d_hat = d_gated * gain
    d_gate = rms * d_hat - hat * (rms * rms * jnp.mean(d_hat * gate_val, axis=1, keepdims=True))
    dgate_ref[...] = (d_gate * mixed * (sigma * (1.0 + gate * (1.0 - sigma)))).astype(low)
    d_mixed = d_gate * act
    dmixed_ref[...] = d_mixed
    sums_ref[1:2, :] += jnp.sum(d_mixed * values, axis=0, keepdims=True)
    dstart_ref[0] = tn(readout, (growth * d_mixed).astype(low))
    dcumul_ref[...] = head_sum(d_mixed * inter, fold_ref[...])


def local_kernel(
    pre_ref, cumul_ref, cumul_t_ref, step_ref, step_t_ref, dmixed_ref, skip_ref,
    dvalues_ref, dstep_ref, dcumul_ref, dbc_ref, rows,
):
    pre = pre_ref[...]
    active = pre * jax.nn.sigmoid(pre)
    inputs_b = active[:, INNER : INNER + NSTATE].astype(low)
    readout = active[:, INNER + NSTATE :].astype(low)
    scores = nt(readout, inputs_b)
    causal = causal_mask()
    mask = first_half(SPAN)
    lane = lax.broadcasted_iota(jnp.int32, (SPAN, SPAN), 1)
    cumul, cumul_t, step_t = cumul_ref[...], cumul_t_ref[...], step_t_ref[...]
    rows[...] = jnp.zeros_like(rows)
    columns = jnp.zeros((SPAN, SPAN), f32)
    d_scores = jnp.zeros((SPAN, SPAN), f32)
    for pair in range(PAIRS):
        cut = slice(pair * SPAN, (pair + 1) * SPAN)
        values = active[:, cut]
        d_mixed = dmixed_ref[:, cut]
        d_low = d_mixed.astype(low)
        d_weights = nt(d_low, diagonal(values, mask))
        weights = []
        for half in range(2):
            h = 2 * pair + half
            decay = decay_of(cumul, cumul_t, h, causal)
            step_row = step_t[h : h + 1, :]
            part = d_weights[:, half * SPAN : (half + 1) * SPAN] * decay
            d_scores = d_scores + part * step_row
            scored = part * scores
            rows[h : h + 1, :] = jnp.sum(scored, axis=0, keepdims=True)
            along = jnp.sum(scored * step_row, axis=1, keepdims=True)
            columns = jnp.where(lane == h, along, columns)
            weights.append((scores * decay * step_row).astype(low))
        back = tn(jnp.concatenate(weights, axis=1), d_low)
        dvalues_ref[:, cut] = (
            jnp.where(mask, back[:SPAN], back[SPAN:]) + skip_ref[:, cut] * d_mixed
        )
    d_step = rows[...].T
    dstep_ref[...] = d_step
    dcumul_ref[...] = columns - d_step * step_ref[...]
    d_low = d_scores.astype(low)
    dbc_ref[:, :NSTATE] = tn(d_low, readout)
    dbc_ref[:, NSTATE:] = nn(d_low, inputs_b)


def finish_kernel(
    pre_ref, cumul_ref, step_ref, sigma_ref, dmixed_ref, start_ref, after_ref,
    dvalues_ref, dstep_ref, dcumul_ref, dinter_ref, dbc_ref, cs_ref, halo_ref, taps_ref,
    head_ref, fold_ref,
    dconv_ref, dpre_ref, edge_ref, sums_ref, heads_ref,
    padded, shifted, lead,
):
    first = pl.program_id(1) == 0

    @pl.when(first & (pl.program_id(0) == 0))
    def _():
        sums_ref[...] = jnp.zeros_like(sums_ref)
        heads_ref[...] = jnp.zeros_like(heads_ref)

    pre = pre_ref[...]
    sigma = jax.nn.sigmoid(pre)
    active = pre * sigma
    values = active[:, :INNER]
    inputs_b = active[:, INNER : INNER + NSTATE].astype(low)
    cumul, step = cumul_ref[...], step_ref[...]
    after = after_ref[0]
    start = start_ref[0]
    after_low = after.astype(low)
    last = cumul[SPAN - 1 : SPAN, :]
    expo_tail = jnp.exp(last - cumul)
    tail = expo_tail * step
    tail_wide = expand(tail)
    fold = fold_ref[...]
    q = nn(inputs_b, after_low)
    d_values = dvalues_ref[...] + tail_wide * q
    d_b = dbc_ref[:, :NSTATE] + nt((tail_wide * values).astype(low), after_low)
    grown = (expand(jnp.exp(cumul)) * dmixed_ref[...]).astype(low)
    d_c = dbc_ref[:, NSTATE:] + nt(grown, start.astype(low))
    d_tail = head_sum(values * q, fold)
    tail_term = d_tail * tail
    d_step = dstep_ref[...] + d_tail * expo_tail
    d_cumul = dcumul_ref[...] + dinter_ref[...] - tail_term
    both = jnp.broadcast_to(jnp.sum(after * start, axis=0, keepdims=True), (8, INNER))
    end = jnp.exp(last) * head_sum(both, fold)[0:1, :] + jnp.sum(
        tail_term, axis=0, keepdims=True
    )
    row = lax.broadcasted_iota(jnp.int32, (SPAN, SPAN), 0)
    column = lax.broadcasted_iota(jnp.int32, (SPAN, SPAN), 1)
    upper = (row <= column).astype(f32)
    d_log = nn(upper, d_cumul, lax.Precision.HIGHEST) + end
    rate = -jnp.exp(head_ref[1:2, :])
    d_pre = (d_step + d_log * rate) * sigma_ref[...]
    d_pre = jnp.where(column < HEADS, d_pre, 0.0)
    dpre_ref[...] = d_pre
    heads_ref[0:1, :] += jnp.sum(d_log * step, axis=0, keepdims=True) * rate
    heads_ref[1:2, :] += jnp.sum(d_pre, axis=0, keepdims=True)
    d_active = jnp.concatenate([d_values, d_b, d_c], axis=1)
    d_conv = d_active * (sigma * (1.0 + pre * (1.0 - sigma)))

    @pl.when(first)
    def _():
        shifted[SPAN:, :] = jnp.zeros((8, XBC), f32)

    @pl.when(jnp.logical_not(first))
    def _():
        shifted[SPAN:, :] = shifted[0:8, :]

    shifted[0:SPAN, :] = d_conv
    padded[0:8, :] = halo_ref[0]
    padded[8:, :] = cs_ref[:, :XBC].astype(f32)
    lead[0:8, :] = jnp.zeros((8, XBC), f32)
    lead[8:, :] = d_conv[0:8, :]
    dconv_ref[...] = sum(
        taps_ref[k : k + 1, :] * shifted[3 - k : 3 - k + SPAN, :] for k in range(CONV)
    )
    edge_ref[0] = sum(taps_ref[k : k + 1, :] * lead[8 - k : 16 - k, :] for k in range(CONV))
    for k in range(CONV):
        sums_ref[k : k + 1, :] += jnp.sum(
            d_conv * padded[5 + k : 5 + k + SPAN, :], axis=0, keepdims=True
        )
    sums_ref[CONV : CONV + 1, :] += jnp.sum(d_conv, axis=0, keepdims=True)


def call(kernel, grid, operands, results, scratch=(), backwards=False, flops=0):
    seqs, spans = grid

    def spec(kind, shape):
        if kind == "all":
            return pl.BlockSpec(shape, lambda b, c: (0,) * len(shape))
        if kind == "seq":
            return pl.BlockSpec((1,) + shape[1:], lambda b, c: (b, 0, 0))

        def at(b, c):
            return b * spans + ((spans - 1 - c) if backwards else c)

        if kind == "span":
            return pl.BlockSpec((1,) + shape[1:], lambda b, c: (at(b, c), 0, 0))
        return pl.BlockSpec((SPAN,) + shape[1:], lambda b, c: (at(b, c), 0))

    arrays = [array for _, array in operands]
    moved = sum(a.size * a.dtype.itemsize for a in arrays)
    return pl.pallas_call(
        kernel,
        grid=grid,
        in_specs=[spec(kind, array.shape) for kind, array in operands],
        out_specs=[spec(kind, shape) for kind, shape, _ in results],
        out_shape=[jax.ShapeDtypeStruct(shape, kept) for _, shape, kept in results],
        scratch_shapes=[pltpu.VMEM(shape, f32) for shape in scratch],
        compiler_params=pltpu.CompilerParams(vmem_limit_bytes=50 * 1024 * 1024),
        cost_estimate=pl.CostEstimate(
            flops=flops, bytes_accessed=2 * moved, transcendentals=0
        ),
    )(*arrays)


def passed_along(block, axis, distance):
    devices = range(lax.axis_size(axis))
    route = [(i - distance, i) for i in devices if i - distance in devices]
    return lax.ppermute(block, axis, route)


def carried_in(decay, state, reverse):
    count = lax.axis_size("ctx")
    place = lax.axis_index("ctx")
    high = lax.reduce_precision(decay, 8, 7)
    extra = jnp.stack([high, decay - high], axis=1)
    sent = jnp.concatenate([state, extra], axis=1).astype(low)
    sent = jnp.pad(sent, ((0, 0), (0, TAIL_ROWS - 2), (0, 0)))
    gathered = lax.all_gather(sent, "ctx")
    entering = jnp.zeros(state.shape, f32)
    for lap in range(count - 1):
        source = count - 1 - lap if reverse else lap
        member = gathered[source].astype(f32)
        scale = member[:, NSTATE : NSTATE + 1] + member[:, NSTATE + 1 : NSTATE + 2]
        passed = scale * entering + member[:, :NSTATE]
        wanted = source > place if reverse else source < place
        entering = jnp.where(wanted, passed, entering)
    return entering


def packed(parts, rows):
    flat = jnp.concatenate([part.reshape(part.shape[0], -1) for part in parts], axis=1)
    return jnp.pad(flat, ((0, 0), (0, rows * SPARE - flat.shape[1]))).reshape(-1, SPARE)


def gather_weights(norm_weight, in_weight, conv_weight, conv_bias, gated_gain, out_weight):
    rows = in_weight.shape[0]
    owners = lax.axis_size("dp")
    members = (norm_weight, conv_weight, conv_bias, gated_gain)
    small = packed([part.reshape(1, -1) for part in members], rows)
    conv_part = lax.all_gather(
        jnp.concatenate([in_weight[:, INNER:], small], axis=1), "dp", axis=0, tiled=True
    )
    gate_part = lax.all_gather(in_weight[:, :INNER], "dp", axis=0, tiled=True)
    out_full = lax.all_gather(out_weight, "dp", axis=0, tiled=True)
    spare = conv_part[:, WIDE - SPARE :].reshape(owners, rows * SPARE)
    cut = 0
    fields = []
    for member in members:
        fields.append(spare[:, cut : cut + member.size])
        cut += member.size
    conv_full = jnp.swapaxes(fields[1].reshape(owners, CONV, -1), 0, 1).reshape(CONV, -1)
    return (
        fields[0].reshape(1, -1).astype(f32),
        conv_part,
        gate_part,
        conv_full.astype(f32),
        fields[2].reshape(1, -1).astype(f32),
        fields[3].reshape(1, -1).astype(f32),
        out_full,
    )


def scattered(grad):
    part = lax.psum_scatter(grad.astype(low), "dp", scatter_dimension=0, tiled=True)
    return lax.psum(part, "ctx").astype(f32)


def on_device(
    tokens,
    norm_weight,
    in_weight,
    conv_weight,
    conv_bias,
    decay_log,
    skip_gain,
    step_bias,
    gated_gain,
    out_weight,
    cotangent,
):
    seqs, length, width = tokens.shape
    count = seqs * length
    spans = length // SPAN
    grid = (seqs, spans)
    blocks = seqs * spans
    owners = lax.axis_size("dp")
    norm_row, conv_part, gate_part, taps, bias, gain, out_full = gather_weights(
        norm_weight, in_weight, conv_weight, conv_bias, gated_gain, out_weight
    )
    stream = tokens.reshape(count, width).astype(f32)
    cotan = cotangent.reshape(count, width)
    inv_rms = lax.rsqrt(jnp.mean(stream * stream, axis=-1, keepdims=True) + epsilon)
    normed = (stream * inv_rms * norm_row).astype(low)
    cs = nn(normed, conv_part).astype(low)
    conv_in = cs[:, :XBC].reshape(seqs, spans, SPAN, XBC)
    ends = conv_in[:, :, SPAN - CONV + 1 :]
    edge = passed_along(ends[:, -1], "ctx", 1)
    halo = jnp.concatenate([edge[:, None], ends[:, :-1]], axis=1).astype(f32)
    halo = jnp.pad(halo, ((0, 0), (0, 0), (8 - CONV + 1, 0), (0, 0))).reshape(blocks, 8, XBC)
    head_rows = jnp.pad(jnp.stack([step_bias, decay_log]), ((0, 6), (0, SPAN - HEADS)))
    skip_row = jnp.repeat(skip_gain, HEADDIM)[None]
    fold = (jnp.arange(INNER)[:, None] // HEADDIM == jnp.arange(SPAN)[None]).astype(low)
    square = ("row", (count, SPAN), f32)
    state_shape = ("span", (blocks, NSTATE, INNER), f32)
    pre, cumul, cumul_t, step, step_t, sigma, update, decay = call(
        prepare_kernel,
        grid,
        [("row", cs), ("span", halo), ("all", taps), ("all", bias), ("all", head_rows)],
        [("row", (count, XBC), f32)] + [square] * 5 + [state_shape, ("span", (blocks, 8, INNER), f32)],
        [(SPAN + 8, XBC)],
        flops=blocks * 60_000_000,
    )
    decay = decay[:, :1].reshape(seqs, spans, 1, INNER)
    update = update.reshape(seqs, spans, NSTATE, INNER)
    total, total_decay = update[:, 0], decay[:, 0]
    for c in range(1, spans):
        total = decay[:, c] * total + update[:, c]
        total_decay = total_decay * decay[:, c]
    entering = carried_in(total_decay[:, 0], total, False)
    partial, = call(
        intra_kernel,
        grid,
        [("row", pre), ("row", cumul), ("row", cumul_t), ("row", step_t), ("all", skip_row)],
        [("row", (count, INNER), f32)],
        flops=blocks * 300_000_000,
    )
    gate_raw = nn(normed, gate_part).astype(low)
    d_gated = nt(cotan, out_full)
    starts = [entering]
    for c in range(spans - 1):
        starts.append(decay[:, c] * starts[-1] + update[:, c])
    starts = jnp.stack(starts, axis=1).reshape(blocks, NSTATE, INNER)
    gated, d_gate_raw, d_mixed, d_start, d_inter, gate_sums = call(
        gate_kernel,
        grid,
        [
            ("row", partial), ("row", pre), ("row", cumul), ("span", starts), ("row", gate_raw),
            ("row", d_gated), ("all", gain), ("all", fold),
        ],
        [
            ("row", (count, INNER), low), ("row", (count, INNER), low),
            ("row", (count, INNER), f32), state_shape, square, ("all", (8, INNER), f32),
        ],
        flops=blocks * 200_000_000,
    )
    d_start = d_start.reshape(seqs, spans, NSTATE, INNER)
    lead = d_start[:, spans - 1]
    for c in range(spans - 2, -1, -1):
        lead = d_start[:, c] + decay[:, c] * lead
    arriving = carried_in(total_decay[:, 0], lead, True)
    out_grad = tn(gated, cotan)
    block_output = (stream + nn(gated, out_full)).astype(low)
    out_part = scattered(out_grad)
    gate_grad = scattered(tn(normed, d_gate_raw))
    d_values, d_step, d_cumul, d_bc = call(
        local_kernel,
        grid,
        [
            ("row", pre), ("row", cumul), ("row", cumul_t), ("row", step), ("row", step_t),
            ("row", d_mixed), ("all", skip_row),
        ],
        [("row", (count, INNER), f32), square, square, ("row", (count, 2 * NSTATE), f32)],
        [(SPAN, SPAN)],
        flops=blocks * 500_000_000,
    )
    after = [arriving]
    for c in range(spans - 1, 0, -1):
        after.append(d_start[:, c] + decay[:, c] * after[-1])
    after = jnp.stack(after[::-1], axis=1).reshape(blocks, NSTATE, INNER)
    d_conv_in, d_step_pre, back_rows, conv_sums, head_sums = call(
        finish_kernel,
        grid,
        [
            ("row", pre), ("row", cumul), ("row", step), ("row", sigma), ("row", d_mixed),
            ("span", starts), ("span", after), ("row", d_values), ("row", d_step),
            ("row", d_cumul), ("row", d_inter), ("row", d_bc), ("row", cs), ("span", halo),
            ("all", taps), ("all", head_rows), ("all", fold),
        ],
        [
            ("row", (count, XBC), f32), square, ("seq", (seqs, 8, XBC), f32),
            ("all", (8, XBC), f32), ("all", (8, SPAN), f32),
        ],
        [(SPAN + 8, XBC), (SPAN + 8, XBC), (16, XBC)],
        backwards=True,
        flops=blocks * 200_000_000,
    )
    heads = jnp.concatenate(
        [
            head_sums[0, :HEADS],
            jnp.sum(gate_sums[1].reshape(HEADS, HEADDIM), axis=1),
            head_sums[1, :HEADS],
        ]
    )
    heads = lax.psum(heads, ("dp", "ctx")).reshape(3, HEADS)
    back_edge = passed_along(back_rows[:, : CONV - 1], "ctx", -1)
    d_conv_in = d_conv_in.reshape(seqs, length, XBC) + jnp.pad(
        back_edge, ((0, 0), (length - CONV + 1, 0), (0, 0))
    )
    d_cs = jnp.concatenate([d_conv_in.reshape(count, XBC), d_step_pre], axis=1).astype(low)
    d_normed = nt(d_cs, conv_part) + nt(d_gate_raw, gate_part)
    norm_grad = jnp.sum(d_normed * stream * inv_rms, axis=0)
    d_hat = d_normed * norm_row
    d_stream = inv_rms * d_hat - stream * inv_rms**3 * jnp.mean(
        d_hat * stream, axis=-1, keepdims=True
    )
    input_grad = (cotan.astype(f32) + d_stream).astype(low)
    members = (
        norm_grad.reshape(owners, -1),
        jnp.swapaxes(conv_sums[:CONV].reshape(CONV, owners, -1), 0, 1).reshape(owners, -1),
        conv_sums[CONV].reshape(owners, -1),
        gate_sums[0].reshape(owners, -1),
    )
    small = packed(members, width // owners)
    conv_grad = scattered(jnp.concatenate([tn(normed, d_cs)[:, : WIDE - SPARE], small], axis=1))
    spare = conv_grad[:, WIDE - SPARE :].reshape(-1)
    cut = 0
    fields = []
    for member in members:
        fields.append(spare[cut : cut + member.shape[1]])
        cut += member.shape[1]
    return (
        block_output.reshape(seqs, length, width),
        input_grad.reshape(seqs, length, width),
        fields[0],
        jnp.concatenate([gate_grad, conv_grad[:, : WIDE - SPARE]], axis=1),
        fields[1].reshape(CONV, -1),
        fields[2],
        heads[0],
        heads[1],
        heads[2],
        fields[3],
        out_part,
    )


def solution(mesh):
    return jax.shard_map(
        on_device,
        mesh=mesh,
        in_specs=(
            P("dp", "ctx", None),
            P("dp"),
            P("dp", None),
            P(None, "dp"),
            P("dp"),
            P(),
            P(),
            P(),
            P("dp"),
            P("dp", None),
            P("dp", "ctx", None),
        ),
        out_specs=(
            P("dp", "ctx", None),
            P("dp", "ctx", None),
            P("dp"),
            P("dp", None),
            P(None, "dp"),
            P("dp"),
            P(),
            P(),
            P(),
            P("dp"),
            P("dp", None),
        ),
        check_vma=False,
    )
```

time: 775 us -> 539 us (0.70)
  blocking collectives: 166 us -> 41.3 us
  waiting for transfers between devices: 222 us -> 331 us
  matrix products: 133 us -> 35.2 us
  local copies, waits for them, and re-layouts: 119 us -> 36.2 us
  other arithmetic: 94.4 us -> 23.3 us
  Pallas kernels: 0 us -> 52.8 us
    all_gather x6 -> x5, waiting for transfers between devices: 34 us -> 170 us  [the longest x1 58.3 us: gather_weights(): lax.all_gather(jnp.concatenate([in_weight[:, INNER:], small], axis=1), 'd...]
    dot_general x36 -> x9, matrix products: 133 us -> 35.2 us  [the longest x3 12.8 us: nt(): lax.dot_general(a, b, (((1,), (1,)), ((), ())), preferred_element_type=f32)]
    unnamed x3 -> x0, blocking collectives: 87.1 us -> none
    pallas_call x0 -> x5, Pallas kernels: none -> 52.8 us  [call(): pl.pallas_call(kernel, grid=grid, in_specs=[spec(kind, array.shape) for k...]
    reduce_scatter x2 -> x1, waiting for transfers between devices: 122 us -> 70 us  [scattered(): lax.psum_scatter(grad.astype(low), 'dp', scatter_dimension=0, tiled=True)]
    reduce_sum x14 -> x2, other arithmetic: 31.9 us -> 0.35 us  [the longest x1 0.23 us: on_device(): jnp.mean(stream * stream, axis=-1, keepdims=True) + epsilon]
    add x33 -> x3, other arithmetic: 30.5 us -> 0.04 us  [carried_in(): scale = member[:, NSTATE:NSTATE + 1] + member[:, NSTATE + 1:NSTATE + 2]]
    unnamed x11, waiting for transfers between devices: 23.1 us -> 51.8 us
  transfers between devices with their start and end apart: 14 -> 11, of which waited for: 6 -> 11; matrix products, arithmetic and copies ran while one was open for 35% -> 13% of each run, Pallas kernels for 0% -> 8%
where the time goes in v1:
time: 539 us; the launch traced here: 538 us
  waiting for transfers between devices  331 us (61%)
  Pallas kernels  52.8 us (10%)
  blocking collectives  41.3 us (8%)
  local copies, waits for them, and re-layouts  36.2 us (7%)
  matrix products  35.2 us (7%)
  other arithmetic  23.3 us (4%)
  between operations  14.5 us (3%)
    reduce_scatter x1, waiting for transfers between devices, scattered(): lax.psum_scatter(grad.astype(low), 'dp', scatter_dimension=0, tiled=True)  70 us
    all_gather x1, waiting for transfers between devices, gather_weights(): lax.all_gather(jnp.concatenate([in_weight[:, INNER:], small], axis=1), 'd...  58.3 us
    pallas_call x5, Pallas kernels, call(): pl.pallas_call(kernel, grid=grid, in_specs=[spec(kind, array.shape) for k...  52.8 us
    unnamed x11, waiting for transfers between devices  51.8 us
    all_gather x1, waiting for transfers between devices, gather_weights(): gate_part = lax.all_gather(in_weight[:, :INNER], 'dp', axis=0, tiled=True)  47.8 us
    psum x1, blocking collectives, on_device(): heads = lax.psum(heads, ('dp', 'ctx')).reshape(3, HEADS)  41.3 us
    psum x1, waiting for transfers between devices, scattered(): return lax.psum(part, 'ctx').astype(f32)  38.1 us
    all_gather x1, waiting for transfers between devices, gather_weights(): out_full = lax.all_gather(out_weight, 'dp', axis=0, tiled=True)  35 us
  transfers between devices with their start and end apart: 11, of which 11 were waited for; matrix products, arithmetic and copies ran while one was open for 13% of the time, Pallas kernels for 8%

profile of v1, /device:TPU:0, one launch (start us, length us, event | category | flops | bytes accessed | tf_op | source)
XLA Modules:
  0.0 537.8 jit_solution(2251793401447328010)
XLA Ops:
  10.3 1.0 slice.190
  13.0 1.7 slice.215
  15.1 58.3 %all-gather.8.cloned.1.call-done = bf16[768,1920]{1,0:T(8,128)(2,1)} async-done(((bf16[96,1920]{1,0:T(8,128)(2,1)}), bf16[768,1920]{1,0:T(8,128)(2,1)}) %all-gather.8.cloned.1.call-update) | async-done | bytes 2949136 | tf_op jit(solution)/shard_map/all_gather | solution.py:361
  73.4 1.0 slice.254
  75.1 3.9 convolution_convert_fusion.3.cs_ref
  79.2 1.3 collective-permute-start
  81.4 6.0 %shard_map.194 = (f32[512,1792]{1,0:T(8,128)}, f32[512,128]{1,0:T(8,128)S(1)}, f32[512,128]{1,0:T(8,128)S(1)}, f32[512,128]{1,0:T(8,128)S(1)}, f32[512,128]{1,0:...) custom-call(bf16[512,1920]{1,0:T(8,128)(2,1)S(1)} %convolution_convert_fusion.3.cs_ref, ...), custom_call_target="tpu_custom_call" | custom-call | flops 240000000 | bytes 4470784 | tf_op jit(solution)/shard_map/pallas_call | solution.py:312
  87.6 2.2 fusion.9
  91.3 35.0 %all-gather.12.cloned.1.call-done = bf16[1536,768]{1,0:T(8,128)(2,1)} async-done(((bf16[192,768]{1,0:T(8,128)(2,1)}), bf16[1536,768]{1,0:T(8,128)(2,1)}) %all-gather.12.cloned.1.call-update) | async-done | bytes 2359312 | tf_op jit(solution)/shard_map/all_gather | solution.py:365
  126.4 4.7 fusion.38.dgated_ref
  131.9 47.8 %all-gather.10.cloned.1.call-done = bf16[768,1536]{1,0:T(8,128)(2,1)} async-done(((bf16[96,1536]{1,0:T(8,128)(2,1)}), bf16[768,1536]{1,0:T(8,128)(2,1)}) %all-gather.10.cloned.1.call-update) | async-done | bytes 2359312 | tf_op jit(solution)/shard_map/all_gather | solution.py:364
  179.8 4.5 convolution_convert_fusion.2.gate_ref
  184.3 4.8 shard_map.195.partial_ref
  189.2 1.7 copy-done.1
  190.9 20.2 %all-gather.14.cloned.1.call-done = bf16[8,144,1536]{2,1,0:T(8,128)(2,1)} async-done(((bf16[2,144,1536]{2,1,0:T(8,128)(2,1)}), bf16[8,144,1536]{2,1,0:T(8,128)(2,1)}) %all-gather.14.cloned.1.call-update) | async-done | bytes 3538960 | tf_op jit(solution)/shard_map/all_gather | solution.py:339
  211.1 2.6 slice_convert_fusion.4
  214.7 1.8 copy.54
  216.6 10.4 %shard_map.196 = (bf16[512,1536]{1,0:T(8,128)(2,1)S(1)}, bf16[512,1536]{1,0:T(8,128)(2,1)S(1)}, f32[512,1536]{1,0:T(8,128)}, f32[4,128,1536]{2,1,0:T(8,128)}, f3...) custom-call(f32[512,1536]{1,0:T(8,128)} %copy-done.1, f32[512,1792]{1,0:T(8,128)} %get-tuple-element.34.pre_ref, ...), custom_call_target="tpu_custom_call" | custom-call | flops 800000000 | bytes 30683136 | tf_op jit(solution)/shard_map/pallas_call | solution.py:312
  227.0 3.3 fusion.4
  230.5 1.0 pad.33
  231.8 14.6 %shard_map.197 = (f32[512,1536]{1,0:T(8,128)}, f32[512,128]{1,0:T(8,128)S(1)}, f32[512,128]{1,0:T(8,128)S(1)}, f32[512,256]{1,0:T(8,128)S(1)}) custom-call(f32[512,1792]{1,0:T(8,128)} %get-tuple-element.34.pre_ref, f32[512,128]{1,0:T(8,128)S(1)} %get-tuple-element.35.cumul_ref, f32[512,128]{1,0:T(8,128)S(1)} %get-tuple-element.36.cumul_t_ref, ...), custom_call_target="tpu_custom_call" | custom-call | flops 2000000000 | bytes 15740928 | tf_op jit(solution)/shard_map/pallas_call | solution.py:312
  246.5 2.8 convolution_convert_fusion.1
  249.3 4.8 fusion.39
  254.2 8.2 %all-gather.16.cloned.1.call-done = bf16[8,144,1536]{2,1,0:T(8,128)(2,1)} async-done(((bf16[2,144,1536]{2,1,0:T(8,128)(2,1)}), bf16[8,144,1536]{2,1,0:T(8,128)(2,1)}) %all-gather.16.cloned.1.call-update) | async-done | bytes 3538960 | tf_op jit(solution)/shard_map/all_gather | solution.py:339
  262.4 2.6 slice_convert_fusion.1
  266.0 1.8 copy.57
  267.9 16.8 %shard_map.198 = (f32[512,1792]{1,0:T(8,128)}, f32[512,128]{1,0:T(8,128)S(1)}, f32[2,8,1792]{2,1,0:T(8,128)S(1)}, f32[8,1792]{1,0:T(8,128)S(1)}, f32[8,128]{1,0:T(8,128)S(1)}) custom-call(f32[512,1792]{1,0:T(8,128)} %get-tuple-element.34.pre_ref, f32[512,128]{1,0:T(8,128)S(1)} %get-tuple-element.35.cumul_ref, f32[512,128]{1,0:T(8,128)S(1)} %get-tuple-element.41.step_ref, ...), custom_call_target="tpu_custom_call" | custom-call | flops 800000000 | bytes 41943040 | tf_op jit(solution)/shard_map/pallas_call | solution.py:312
  284.7 1.5 collective-permute-start.1
  286.6 1.2 collective-permute-done.1
  287.9 2.4 add_convert_fusion
  291.1 1.1 copy-done.24
  292.2 3.2 fusion.20
  296.3 3.2 fusion.21
  299.7 1.8 pad_maximum_fusion.2
  301.4 4.6 copy.63
  306.2 1.4 copy-done.4
  307.5 4.0 convolution_convert_fusion
  312.6 4.0 fusion.13
  316.5 18.3 %reduce-scatter.12.cloned.1.call-done = bf16[96,1536]{1,0:T(8,128)(2,1)} async-done(((bf16[768,1536]{1,0:T(8,128)(2,1)}), bf16[96,1536]{1,0:T(8,128)(2,1)}) %reduce-scatter.12.cloned.1.call-update) | async-done | bytes 294928
  334.8 1.9 copy.66
  336.8 41.3 %psum.30 = f32[72]{0:T(128)S(1)} all-reduce(f32[72]{0:T(128)S(1)} %pad_maximum_fusion.12), channel_id=1, replica_groups=mesh['dp'=8,'ctx'=4] {'dp','ctx'}, use_global_device_ids=true, to_apply=%region_8.9 | all-reduce | flops 72 | bytes 576 | tf_op jit(solution)/shard_map/psum | solution.py:515
  378.7 32.7 %reduce-scatter.10.cloned.1.call-done = bf16[96,1920]{1,0:T(8,128)(2,1)} async-done(((bf16[768,1920]{1,0:T(8,128)(2,1)}), bf16[96,1920]{1,0:T(8,128)(2,1)}) %reduce-scatter.10.cloned.1.call-update) | async-done | bytes 368656
  411.4 2.0 copy.64
  413.3 70.0 %reduce-scatter.8.cloned.1.call-done = bf16[192,768]{1,0:T(8,128)(2,1)} async-done(((bf16[1536,768]{1,0:T(8,128)(2,1)}), bf16[192,768]{1,0:T(8,128)(2,1)}) %reduce-scatter.8.cloned.1.call-update) | async-done | bytes 294928 | tf_op jit(solution)/shard_map/reduce_scatter | solution.py:385
  483.4 2.5 fusion.17
  485.9 38.1 %all-reduce.10.cloned.1.call-done = (bf16[96,1920]{0,1:T(8,128)(2,1)}, bf16[96,1536]{0,1:T(8,128)(2,1)}, bf16[192,768]{1,0:T(8,128)(2,1)}) async-done(((bf16[96,1920]{0,1:T(8,128)(2,1)}, bf16[96,1536]{0,1:T(8,128)(2,1)}, bf16[192,768]{1,0:T(8,128)(2,1)}), (bf16[96,1920]{0,1:T(8,128)(2,1)}, bf16[96,1536]{0,1:T(8,128)(2,1)}, bf16[192,768]{1,0:T(8,128)(2,1)})) %all-reduce.10.cloned.1.call-update) | async-done | bytes 958480 | tf_op jit(solution)/shard_map/psum | solution.py:386
  524.8 1.1 slice.298
  528.2 1.6 copy.62
  (156 shorter events, 20.2 us)
Async XLA Ops:
  7.2 7.6 %copy-start.9 = (bf16[2,256,768]{2,1,0:T(8,128)(2,1)S(1)}, bf16[2,256,768]{2,1,0:T(8,128)(2,1)}, u32[]{:S(2)}) copy-start(bf16[2,256,768]{2,1,0:T(8,128)(2,1)} %param.11) | copy-start | bytes 2359300
  7.2 66.2 %all-gather.8.cloned.1.call-start = ((), (), s32[]{:S(2)}) async-start(), calls=%async_computation.3 | async-start | bytes 3317760 | tf_op jit(solution)/shard_map/all_gather | solution.py:361
  11.3 3.7 copy-start.21
  11.4 3.7 copy-start.22
  12.2 114.1 %all-gather.12.cloned.1.call-start = ((), (), s32[]{:S(2)}) async-start(), calls=%async_computation.5 | async-start | bytes 2654208 | tf_op jit(solution)/shard_map/all_gather | solution.py:365
  13.0 166.8 %all-gather.10.cloned.1.call-start = ((), (), s32[]{:S(2)}) async-start(), calls=%async_computation.4 | async-start | bytes 2654208 | tf_op jit(solution)/shard_map/all_gather | solution.py:364
  14.7 196.4 %all-gather.14.cloned.1.call-start = ((), (), s32[]{:S(2)}) async-start(), calls=%async_computation.7 | async-start | bytes 4423680 | tf_op jit(solution)/shard_map/all_gather | solution.py:339
  74.7 5.8 %copy-start.19 = (bf16[8,9984]{1,0:T(8,128)(2,1)}, bf16[8,9984]{1,0:T(8,128)(2,1)S(1)}, u32[]{:S(2)}) copy-start(bf16[8,9984]{1,0:T(8,128)(2,1)S(1)} %reshape.285) | copy-start | bytes 479236
  75.1 3.9 copy-start.14
  79.0 2.4 copy-start
  79.2 2.1 collective-permute-start
  89.8 1.1 copy-start.23
  89.8 36.5 %copy-start.13 = (bf16[2,256,768]{2,1,0:T(8,128)(2,1)S(1)}, bf16[2,256,768]{2,1,0:T(8,128)(2,1)}, u32[]{:S(2)}) copy-start(bf16[2,256,768]{2,1,0:T(8,128)(2,1)} %param.21) | copy-start | bytes 2359300
  90.8 171.5 %all-gather.16.cloned.1.call-start = ((), (), s32[]{:S(2)}) async-start(), calls=%async_computation.8 | async-start | bytes 4423680 | tf_op jit(solution)/shard_map/all_gather | solution.py:339
  189.2 1.7 copy-start.1
  211.1 2.7 copy-start.7
  227.0 3.3 copy-start.3
  227.0 3.4 copy-start.5
  227.0 4.7 copy-start.2
  231.5 103.4 %reduce-scatter.12.cloned.1.call-start = ((), (), s32[]{:S(2)}) async-start(), calls=%async_computation.10 | async-start | bytes 2654208
  231.8 14.6 %copy-start.6 = (bf16[512,1536]{1,0:T(8,128)(2,1)S(1)}, bf16[512,1536]{1,0:T(8,128)(2,1)}, u32[]{:S(2)}) copy-start(bf16[512,1536]{1,0:T(8,128)(2,1)} %copy-done.5) | copy-start | bytes 4718596
  231.8 14.6 %copy-start.15 = (bf16[512,768]{1,0:T(8,128)(2,1)S(1)}, bf16[512,768]{1,0:T(8,128)(2,1)}, u32[]{:S(2)}) copy-start(bf16[512,768]{1,0:T(8,128)(2,1)} %copy-done.14) | copy-start | bytes 2359300
  249.3 162.1 %reduce-scatter.10.cloned.1.call-start = ((), (), s32[]{:S(2)}) async-start(), calls=%async_computation.9 | async-start | bytes 3317760
  262.4 2.7 copy-start.8
  284.7 3.1 collective-permute-start.1
  287.8 2.4 copy-start.10
  287.9 3.2 copy-start.20
  287.9 4.4 copy-start.24
  290.3 5.1 copy-start.11
  292.2 4.0 copy-start.16
  306.1 1.4 copy-start.4
  306.1 177.3 %reduce-scatter.8.cloned.1.call-start = ((), (), s32[]{:S(2)}) async-start(), calls=%async_computation.6 | async-start | bytes 2654208 | tf_op jit(solution)/shard_map/reduce_scatter | solution.py:385
  311.5 212.5 %all-reduce.10.cloned.1.call-start = ((), (), s32[]{:S(2)}) async-start(), calls=%async_computation.11 | async-start | bytes 2359296 | tf_op jit(solution)/shard_map/psum | solution.py:386
  316.5 166.9 %copy-start.12 = (f32[512,768]{1,0:T(8,128)S(1)}, f32[512,768]{1,0:T(8,128)}, u32[]{:S(2)}) copy-start(f32[512,768]{1,0:T(8,128)} %get-tuple-element.116) | copy-start | bytes 4718596
  524.0 3.9 copy-start.17
  528.1 2.3 copy-start.18
Sparse Core Ops, SparseCore 0:
  12.3 61.0 all-gather.7
  75.6 50.7 all-gather.11
  129.1 50.5 all-gather.9
  181.8 29.2 all-gather.13
  231.6 30.7 all-gather.15
  265.7 69.0 reduce-scatter.11
  338.4 72.9 reduce-scatter.9
  415.2 68.0 reduce-scatter.7
  487.2 36.7 all-reduce.9
